TPU v7x, 256 devices: a whole 4x4x8 slice. The times are simulated.
256 devices in a mesh: dp: 32 (over x_hi, z, core), tensor: 8 (over y, x_lo).
Axes of the slice: x: 4 (x_hi: 2, x_lo: 2; x = x_hi * 2 + x_lo), y: 4, z: 8, core: 2. Of those that a mesh axis runs over, the one named last changes fastest.
Arguments:
- layer_input: bfloat16 [24576, 5120], P('dp', 'tensor'), may hold values from -6 to 6
- queries: bfloat16 [24576, 5120], P('dp', 'tensor'), may hold values from -160 to 160
- projected_key_value: bfloat16 [24576, 8, 256], P('dp', 'tensor'), may hold values from -6 to 6
- output_grad: bfloat16 [24576, 5120], P('dp', 'tensor'), may hold values from -6 to 6
- projection: bfloat16 [5120, 8, 256], P(None, 'tensor'), may hold values from -0.078125 to 0.078125
- moment: bfloat16 [32, 5120, 8, 256], P('dp', None, 'tensor'), may hold values from -6 to 6
- rewards: float32 [64], P('dp'), may hold values from -16 to 16
- groups: int32 [64], P('dp'), may hold values from 0 to 7, as said below
- lengths: int32 [64], replicated, may hold values from 1 to 384, 8192 in all
- assignment: int32 [64], replicated, may hold values from 0 to 31, as said below
- sync_flags: int32 [8], replicated, may hold values from 0 to 1, as said below
Outputs:
- query_grad: bfloat16 [24576, 5120], P('dp', 'tensor')
- input_grad: bfloat16 [24576, 5120], P('dp', 'tensor')
- moment_out: bfloat16 [32, 5120, 8, 256], P('dp', None, 'tensor')
Inputs may be any that keep to these rules, and one draw needn't show every extreme that they name: The lengths add up to 8192 and the longest is exactly 384. `groups`: each prompt has exactly 8 responses. `assignment`: response r goes to replica r // 2 or to replica (r // 2 + 32 // 2) % 32; exactly 1 of the responses of every replica go to the second. `sync_flags`: exactly 4 of the flags are 1.
All inputs are finite; a program needn't handle non-finite values.
Results may differ from a plain program's by a relative error of at most 0.017.
Values may be sent and summed in bfloat16 or wider, within the bound.
A program may use at most 128 MiB of HBM per device.

v0:
```python
import math

import jax
import jax.numpy as jnp
from jax import lax
from jax.sharding import PartitionSpec as P

QUERY_HEADS = 40
KEY_VALUE_HEADS = 8
HEAD_SIZE = 128
GROUP = 8
NSYNC = 8


def swapped(value, axis, apart):
    mask = 2**apart
    pairs = [(source, source ^ mask) for source in range(lax.axis_size(axis))]
    return lax.ppermute(value, axis, pairs)


def attention_back(queries, projected_key_value, gradient_scaled, seq_lengths):
    response_list = queries.shape[0]
    token_slot_length = queries.shape[1]
    key_value_head = projected_key_value.shape[2]
    reshaped_query = queries.reshape(
        response_list, token_slot_length, key_value_head, QUERY_HEADS // KEY_VALUE_HEADS, HEAD_SIZE
    )
    reshaped_gradient = gradient_scaled.reshape(
        response_list, token_slot_length, key_value_head, QUERY_HEADS // KEY_VALUE_HEADS, HEAD_SIZE
    )
    key_rows = projected_key_value[..., :HEAD_SIZE]
    value_rows = projected_key_value[..., HEAD_SIZE:]
    score_scale = 1.0 / math.sqrt(HEAD_SIZE)
    scores = (
        jnp.einsum(
            "rtgjd,rsgd->rgjts", reshaped_query, key_rows, preferred_element_type=jnp.float32
        )
        * score_scale
    )
    position = jnp.arange(token_slot_length)
    allowed = (position[None, None, :] <= position[None, :, None]) & (
        position[None, None, :] < seq_lengths[:, None, None]
    )
    scores = jnp.where(allowed[:, None, None], scores, -jnp.inf)
    attention = jnp.exp(scores - jnp.max(scores, axis=-1, keepdims=True))
    attention = attention / jnp.sum(attention, axis=-1, keepdims=True)
    value_scores = jnp.einsum(
        "rtgjd,rsgd->rgjts", reshaped_gradient, value_rows, preferred_element_type=jnp.float32
    )
    row_delta = jnp.sum(attention * value_scores, axis=-1, keepdims=True)
    score_grads = (attention * (value_scores - row_delta)).astype(jnp.bfloat16)
    rounded = attention.astype(jnp.bfloat16)
    query_gradient = (
        jnp.einsum("rgjts,rsgd->rtgjd", score_grads, key_rows, preferred_element_type=jnp.float32)
        * score_scale
    ).astype(jnp.bfloat16)
    grad_key = (
        jnp.einsum(
            "rgjts,rtgjd->rsgd", score_grads, reshaped_query, preferred_element_type=jnp.float32
        )
        * score_scale
    ).astype(jnp.bfloat16)
    grad_value = jnp.einsum(
        "rgjts,rtgjd->rsgd", rounded, reshaped_gradient, preferred_element_type=jnp.float32
    ).astype(jnp.bfloat16)
    return (
        query_gradient.reshape(response_list, token_slot_length, -1),
        jnp.concatenate([grad_key, grad_value], axis=-1),
    )


def project_back(key_value_gradient, projection):
    flat_rows = key_value_gradient.reshape(-1, projection.shape[1] * projection.shape[2])
    weights = projection.reshape(projection.shape[0], -1)
    partial_rows = lax.dot_general(
        flat_rows, weights, (((1,), (1,)), ((), ())), preferred_element_type=jnp.float32
    )
    summed = lax.psum_scatter(
        partial_rows.astype(jnp.bfloat16), "tensor", scatter_dimension=1, tiled=True
    )
    return summed


def weight_grads(row_inputs, row_grads):
    token_count = row_grads.shape[0]
    flat_grads = row_grads.reshape(token_count, -1)
    gathered = lax.dot_general(
        lax.all_gather(row_inputs, "tensor", axis=1, tiled=True),
        flat_grads,
        (((0,), (0,)), ((), ())),
        preferred_element_type=jnp.float32,
    )
    return gathered.reshape(gathered.shape[0], row_grads.shape[1], row_grads.shape[2])


def shards(
    layer_input,
    queries,
    projected_key_value,
    output_grad,
    projection,
    moment,
    rewards,
    groups,
    lengths,
    assignment,
    sync_flags,
):
    replicas = lax.axis_size("dp")
    replica_index = lax.axis_index("dp")
    response_list = rewards.shape[0]
    tokens = layer_input.shape[0]
    token_slot_length = tokens // response_list
    key_value_head = projected_key_value.shape[1]
    feature_width = layer_input.shape[1]
    query_width = queries.shape[1]
    group_count = response_list * replicas // GROUP
    member = (groups[:, None] == jnp.arange(group_count)[None, :]).astype(jnp.float32)
    group_sums = lax.psum(jnp.sum(member * rewards[:, None], axis=0), "dp")
    advantage = rewards - jnp.sum(member * (group_sums / GROUP)[None, :], axis=1)
    own_lengths = lax.dynamic_slice_in_dim(lengths, replica_index * response_list, response_list)
    live_rows = jnp.arange(token_slot_length)[None, :] < own_lengths[:, None]
    scaled = advantage[:, None, None] * output_grad.reshape(
        response_list, token_slot_length, query_width
    ).astype(jnp.float32)
    gradient_scaled = jnp.where(live_rows[:, :, None], scaled, 0.0).astype(jnp.bfloat16)
    own_moving = (
        lax.dynamic_slice_in_dim(assignment, replica_index * response_list, response_list)
        != replica_index
    ).astype(jnp.int32)
    slot_order = jnp.argsort(own_moving, stable=True)
    kept_count = response_list - response_list // 2
    partner_bit = replicas.bit_length() - 2
    slot_inputs = layer_input.reshape(response_list, token_slot_length, feature_width)
    slot_queries = queries.reshape(response_list, token_slot_length, query_width)
    slot_pairs = projected_key_value.reshape(
        response_list, token_slot_length, key_value_head, 2 * HEAD_SIZE
    )
    partner = (replica_index + replicas // 2) % replicas
    their_lengths = lax.dynamic_slice_in_dim(lengths, partner * response_list, response_list)
    their_moving = (
        lax.dynamic_slice_in_dim(assignment, partner * response_list, response_list) != partner
    ).astype(jnp.int32)
    their_order = jnp.argsort(their_moving, stable=True)
    post_lengths = jnp.concatenate(
        [own_lengths[slot_order][:kept_count], their_lengths[their_order][kept_count:]]
    )
    bundle = jnp.concatenate(
        [
            slot_inputs,
            slot_queries,
            gradient_scaled,
            slot_pairs.reshape(response_list, token_slot_length, -1),
        ],
        axis=2,
    )[slot_order]
    arrived = swapped(bundle[kept_count:], "dp", partner_bit)
    worked = jnp.concatenate([bundle[:kept_count], arrived], axis=0)
    grad_start = feature_width + query_width
    pair_start = feature_width + 2 * query_width
    query_gradient, key_value_gradient = attention_back(
        worked[:, :, feature_width:grad_start],
        worked[:, :, pair_start:].reshape(
            response_list, token_slot_length, key_value_head, 2 * HEAD_SIZE
        ),
        worked[:, :, grad_start:pair_start],
        post_lengths,
    )
    grad_input = project_back(key_value_gradient, projection)
    results = jnp.concatenate(
        [query_gradient, grad_input.reshape(response_list, token_slot_length, feature_width)],
        axis=2,
    )
    returned = swapped(results[kept_count:], "dp", partner_bit)
    restored = jnp.concatenate([results[:kept_count], returned], axis=0)[jnp.argsort(slot_order)]
    query_grad = restored[:, :, :query_width].reshape(tokens, query_width)
    input_grad = restored[:, :, query_width:].reshape(tokens, feature_width)
    weight_gradient = weight_grads(
        worked[:, :, :feature_width].reshape(tokens, feature_width),
        key_value_gradient.reshape(tokens, key_value_head, 2 * HEAD_SIZE),
    )
    updated_state = (0.9 * moment[0].astype(jnp.float32) + 0.1 * weight_gradient).astype(
        jnp.bfloat16
    )
    block_rows = updated_state.shape[0] // NSYNC
    summed = lax.psum(updated_state, "dp").astype(jnp.float32)
    synced_rows = jnp.repeat(sync_flags == 1, block_rows)
    moment_out = jnp.where(
        synced_rows[:, None, None], (summed / replicas).astype(jnp.bfloat16), updated_state
    )
    return (query_grad, input_grad, moment_out[None])


def solution(mesh):
    return jax.shard_map(
        shards,
        mesh=mesh,
        in_specs=(
            P("dp", "tensor"),
            P("dp", "tensor"),
            P("dp", "tensor", None),
            P("dp", "tensor"),
            P(None, "tensor", None),
            P("dp", None, "tensor", None),
            P("dp"),
            P("dp"),
            P(),
            P(),
            P(),
        ),
        out_specs=(P("dp", "tensor"), P("dp", "tensor"), P("dp", None, "tensor", None)),
        check_vma=False,
    )
```

profile of v0, /device:TPU:1, one launch (start us, length us, event | category | flops | bytes accessed | tf_op | source)
XLA Modules:
  0.0 760.0 jit_solution(9779404894831122697)
XLA Ops:
  10.3 68.9 %psum.14 = f32[8]{0:T(128)S(1)} all-reduce(f32[8]{0:T(128)S(1)} %select_reduce_fusion.1), channel_id=1, replica_groups=mesh['dp'=32,'tensor'=8] {'dp'}, use_global_device_ids=true, to_apply=%region_1.0 | all-reduce | flops 8 | bytes 64 | tf_op jit(solution)/shard_map/psum | solution.py:119
  82.4 3.1 pad_maximum_fusion
  85.5 4.6 gather_fusion
  92.6 34.0 %collective-permute-done = bf16[1,384,2176]{2,1,0:T(8,128)(2,1)S(1)} collective-permute-done((bf16[1,384,2176]{2,1,0:T(8,128)(2,1)S(1)}, bf16[1,384,2176]{2,1,0:T(8,128)(2,1)S(1)}, u32[]{:S(2)}, u32[]{:S(2)}) %collective-permute-start) | collective-permute-done | bytes 1671200 | tf_op jit(solution)/shard_map/ppermute | solution.py:18
  132.6 2.3 copy.48
  134.9 2.2 copy.50
  140.9 2.2 fusion.3
  149.9 5.3 convolution_convert_fusion
  155.2 10.7 %copy.72 = bf16[768,5120]{0,1:T(8,128)(2,1)} copy(bf16[768,5120]{1,0:T(8,128)(2,1)} %convolution_convert_fusion) | data formatting | bytes 15728640
  166.2 124.1 %all-gather.2.cloned.1.call-done = bf16[768,5120]{1,0:T(8,128)(2,1)} async-done(((bf16[768,640]{1,0:T(8,128)(2,1)}), bf16[768,5120]{1,0:T(8,128)(2,1)}) %all-gather.2.cloned.1.call-update) | async-done | bytes 7864336 | tf_op jit(solution)/shard_map/all_gather | solution.py:88
  290.3 7.8 %fusion.2 = bf16[5120,1,256]{2,0,1:T(8,128)(2,1)} fusion(bf16[768,5120]{1,0:T(8,128)(2,1)} %all-gather.2.cloned.1.call-done, bf16[768,256]{1,0:T(8,128)(2,1)S(1)} %bitcast.139, bf16[1,5120,1,256]{3,1,2,0:T(8,128)(2,1)} %param.16), kind=kOutput, calls=%fused_computation.8 | convolution fusion | flops 2019819520 | bytes 13500416 | tf_op jit(solution)/shard_map/dot_general | solution.py:87
  298.9 3.5 multiply_convert_fusion.1
  302.4 153.3 %reduce-scatter.4.cloned.1.call-done = bf16[640,768]{1,0:T(8,128)(2,1)} async-done(((bf16[5120,768]{1,0:T(8,128)(2,1)}), bf16[640,768]{1,0:T(8,128)(2,1)}) %reduce-scatter.4.cloned.1.call-update) | async-done | bytes 983056
  455.7 2.2 copy.73
  457.9 2.2 copy.57
  460.2 3.0 fusion.31
  463.1 2.4 collective-permute-start.1
  465.5 268.2 %all-reduce.2.cloned.1.call-done = bf16[5120,1,256]{2,0,1:T(8,128)(2,1)} async-done(((bf16[5120,1,256]{2,0,1:T(8,128)(2,1)}), bf16[5120,1,256]{2,0,1:T(8,128)(2,1)}) %all-reduce.2.cloned.1.call-update) | async-done | bytes 2621456 | tf_op jit(solution)/shard_map/psum | solution.py:186
  733.8 5.9 fusion.14
  739.7 2.7 pad_maximum_fusion.1
  742.4 3.6 gather_fusion.3
  746.0 3.0 fusion.37
  749.0 2.2 copy.58
  751.2 2.2 copy.59
  (64 shorter events, 26.3 us)
Async XLA Ops:
  7.2 142.7 %copy-start = (bf16[5120,1,256]{2,0,1:T(8,128)(2,1)S(1)}, bf16[5120,1,256]{2,0,1:T(8,128)(2,1)}, u32[]{:S(2)}) copy-start(bf16[5120,1,256]{2,0,1:T(8,128)(2,1)} %param.15) | copy-start | bytes 7864324
  7.2 283.1 %all-gather.2.cloned.1.call-start = ((), (), s32[]{:S(2)}) async-start(), calls=%async_computation.1 | async-start | bytes 8847360 | tf_op jit(solution)/shard_map/all_gather | solution.py:88
  92.2 34.3 %copy-start.2 = (bf16[1,384,2176]{2,1,0:T(8,128)(2,1)}, bf16[1,384,2176]{2,1,0:T(8,128)(2,1)S(1)}, u32[]{:S(2)}) copy-start(bf16[1,384,2176]{2,1,0:T(8,128)(2,1)S(1)} %get-tuple-element.12) | copy-start | bytes 5013508
  92.2 34.3 %collective-permute-start = (bf16[1,384,2176]{2,1,0:T(8,128)(2,1)S(1)}, bf16[1,384,2176]{2,1,0:T(8,128)(2,1)S(1)}, u32[]{:S(2)}, u32[]{:S(2)}) collective-permute-start(bf16[1,384,2176]{2,1,0:T(8,128)(2,1)S(1)} %get-tuple-element.13), channel_id=1, source_target_pairs={{0,128},{8,136},{16,144},{24,152},{32,160},{40,168},{48,176},{56,1... | collective-permute-start | bytes 5013512 | tf_op jit(solution)/shard_map/ppermute | solution.py:18
  126.5 2.1 copy-start.4
  128.7 327.0 %reduce-scatter.4.cloned.1.call-start = ((), (), s32[]{:S(2)}) async-start(), calls=%async_computation.3 | async-start | bytes 8847360
  137.1 1.4 copy-start.3
  139.6 1.3 copy-start.6
  144.9 3.0 copy-start.1
  165.9 132.8 %copy-start.7 = (s32[8]{0:T(128)S(1)}, s32[8]{0:T(128)}, u32[]{:S(2)}) copy-start(s32[8]{0:T(128)} %param.21) | copy-start | bytes 100
  165.9 567.9 %all-reduce.2.cloned.1.call-start = ((), (), s32[]{:S(2)}) async-start(), calls=%async_computation.2 | async-start | bytes 5242880 | tf_op jit(solution)/shard_map/psum | solution.py:186
  463.1 276.5 %collective-permute-start.1 = (bf16[1,384,1280]{1,2,0:T(8,128)(2,1)}, bf16[1,384,1280]{1,2,0:T(8,128)(2,1)}, u32[]{:S(2)}, u32[]{:S(2)}) collective-permute-start(bf16[1,384,1280]{1,2,0:T(8,128)(2,1)} %get-tuple-element.17), channel_id=1, source_target_pairs={{0,128},{8,136},{16,144},{24,152},{32,160},{40,168},{48,176},{56,1... | collective-permute-start | bytes 2949128 | tf_op jit(solution)/shard_map/ppermute | solution.py:18
  733.8 5.9 copy-start.5
Sparse Core Ops, SparseCore 0:
  128.8 161.4 all-gather.1
  292.8 162.8 reduce-scatter.3
  458.9 274.8 all-reduce.1
where the time goes:
time: 761 us; the launch traced here: 760 us
  waiting for transfers between devices  580 us (76%)
  blocking collectives  68.9 us (9%)
  local copies, waits for them, and re-layouts  42.1 us (6%)
  other arithmetic  29.2 us (4%)
  matrix products  22.9 us (3%)
  between operations  13.9 us (2%)
    psum x1, waiting for transfers between devices, shards(): summed = lax.psum(updated_state, 'dp').astype(jnp.float32)  268 us
    unnamed x4, waiting for transfers between devices  153 us
    all_gather x1, waiting for transfers between devices, weight_grads(): lax.all_gather(row_inputs, 'tensor', axis=1, tiled=True)  124 us
    psum x1, blocking collectives, shards(): group_sums = lax.psum(jnp.sum(member * rewards[:, None], axis=0), 'dp')  68.9 us
    ppermute x2, waiting for transfers between devices, swapped(): return lax.ppermute(value, axis, pairs)  34 us
  transfers between devices with their start and end apart: 5, of which 4 were waited for; matrix products, arithmetic and copies ran while one was open for 8% of the time, Pallas kernels for 0%

commit v1 on v0

v1 whole, which is shorter than its diff:
```python
import functools
import math

import jax
import jax.numpy as jnp
from jax import lax
from jax.experimental import pallas as pl
from jax.experimental.pallas import tpu as pltpu
from jax.sharding import PartitionSpec as P

HEAD = 128
HEADS = 5
TENSOR = 8
ZS = 8
REPLICAS = 32
SLOTS = 384
WIDTH = 640
GROUP = 8
SYNCED = 4
CHUNKS = ((0, 640),)
SEMS = 128
BF = jnp.bfloat16
F32 = jnp.float32
MESH = pl.DeviceIdType.MESH


def dot(a, b, ca, cb):
    return lax.dot_general(a, b, (((ca,), (cb,)), ((), ())), preferred_element_type=F32)


def kernel(*refs):
    nc = len(CHUNKS)
    refs = list(refs)
    take = lambda n: [refs.pop(0) for _ in range(n)]
    x_hbm, q_hbm, kv_hbm, do_hbm, proj_hbm, mom_hbm = take(6)
    rewards, groups, lengths, assignment, flags = take(5)
    dq_out, ig_out, mom_out = take(3)
    xv, qv, kvv, dov, pv, pg, mv, xg, xm, kvown, kvg, kva, kvm, st, dqf, dkv = take(16)
    rt = take(1)[0]
    ar = [dict(zip(("sc", "cr", "ab", "zr", "xs", "xr", "mn"), take(7))) for _ in range(nc)]
    ss, rs, ls = take(3)

    dp = lax.axis_index("dp")
    t = lax.axis_index("tensor")
    xh, z, core = dp // 16, lax.rem(dp // 2, ZS), lax.rem(dp, 2)
    y, xl = t // 2, lax.rem(t, 2)

    def dev(xh_=xh, z_=z, core_=core, t_=t):
        return (xh_ * 16 + z_ * 2 + core_, t_)

    def ring(a, i, n):
        return lax.rem(a + (i + n), n)

    yt = lambda i, xl_=xl: ring(y, i, 4) * 2 + xl_
    pair_t = y * 2 + (1 - xl)
    pair = dev(t_=pair_t)
    yp, ym = dev(t_=yt(1)), dev(t_=yt(-1))
    sibling = dev(core_=1 - core)
    partner = dev(xh_=1 - xh)
    across = dev(xh_=1 - xh, t_=pair_t)
    tpeer = [dev(t_=ring(t, i, TENSOR)) for i in range(1, TENSOR)]
    zpeer = [dev(z_=ring(z, i, ZS)) for i in range(1, ZS)]

    counter = [0]
    sent = []

    def xfer(src, there, here, to):
        i = counter[0]
        counter[0] += 1
        copy = pltpu.make_async_remote_copy(src, there, ss.at[i], rs.at[i], device_id=to, device_id_type=MESH)
        copy.start()
        sent.append(copy)
        return pltpu.make_async_remote_copy(src, here, ss.at[i], rs.at[i], device_id=to, device_id_type=MESH)

    def local(src, dst, i):
        copy = pltpu.make_async_copy(src, dst, ls.at[i])
        copy.start()
        return copy

    lx = local(x_hbm, xv, 0)
    lproj = [local(proj_hbm.at[:, :, pl.ds(h * 128, 128)], pv.at[h], 1 + h) for h in range(2)]
    lkv = local(kv_hbm, kvv, 3)
    lq = local(q_hbm, qv, 4)
    ldo = local(do_hbm, dov, 5)
    lmom = local(mom_hbm, mv, 6)

    barrier = pltpu.get_barrier_semaphore()
    others = [sibling, partner, across] + tpeer + zpeer
    for other in others:
        pl.semaphore_signal(barrier, inc=1, device_id=other, device_id_type=MESH)

    moving = [assignment[2 * dp + j] != dp for j in range(2)]
    gone = jnp.where(moving[0], 0, 1)
    kept = 1 - gone

    group_row = lax.broadcasted_iota(jnp.int32, (8, 128), 0)
    tile = jnp.zeros((8, 128), F32)
    for j in range(2):
        tile = tile + jnp.where(group_row == groups[j], rewards[j], 0.0)
    rt[0] = tile

    lx.wait()
    xm[...] = xv[gone]
    xg[t, 0] = xv[kept]
    pl.semaphore_wait(barrier, len(others))

    HALF = SLOTS // 2
    top, low = pl.ds(0, HALF), pl.ds(HALF, HALF)

    def gather_kept(c0, cw):
        cols = pl.ds(c0, cw)
        at = lambda idx, rows=pl.ds(0, SLOTS): xg.at[idx, 0, rows, cols]
        own = at(t)
        a = xfer(own, own, at(pair_t), pair)
        b = xfer(own, own, at(yt(-1)), yp)
        c = xfer(own, own, at(yt(1)), ym)
        yield
        b.wait_recv()
        f = xfer(at(yt(-1), top), at(yt(-1), top), at(yt(2), top), yp)
        d = xfer(at(yt(-1)), at(yt(-1)), at(yt(-1, 1 - xl)), pair)
        c.wait_recv()
        g = xfer(at(yt(1), low), at(yt(1), low), at(yt(2), low), ym)
        e = xfer(at(yt(1)), at(yt(1)), at(yt(1, 1 - xl)), pair)
        yield
        f.wait_recv()
        g.wait_recv()
        h = xfer(at(yt(2)), at(yt(2)), at(yt(2, 1 - xl)), pair)
        yield
        for r in (a, d, e, h):
            r.wait_recv()

    def gather_moved(c0, cw):
        cols = pl.ds(c0, cw)
        at = lambda idx, rows=pl.ds(0, SLOTS): xg.at[idx, 1, rows, cols]
        a = xfer(xm.at[:, cols], at(t), at(pair_t), across)
        yield
        a.wait_recv()
        b = xfer(at(pair_t), at(pair_t), at(t), pair)
        up = [xfer(at(pair_t), at(pair_t), at(yt(-1, 1 - xl)), yp)]
        down = [xfer(at(pair_t), at(pair_t), at(yt(1, 1 - xl)), ym)]
        yield
        b.wait_recv()
        up.append(xfer(at(t), at(t), at(yt(-1)), yp))
        down.append(xfer(at(t), at(t), at(yt(1)), ym))
        last = []
        for i, x_ in ((0, 1 - xl), (1, xl)):
            yield
            up[i].wait_recv()
            p = at(yt(-1, x_), top)
            last.append(xfer(p, p, at(yt(2, x_), top), yp))
            down[i].wait_recv()
            p = at(yt(1, x_), low)
            last.append(xfer(p, p, at(yt(2, x_), low), ym))
        yield
        for r in last:
            r.wait_recv()

    SH = WIDTH // ZS

    def gather_projection():
        for cp in lproj:
            cp.wait()
        mine = pl.ds(pl.multiple_of(z * SH, 16), SH)
        pg[core, t, mine] = pv[core, t, mine]
        got = []
        for i in range(1, TENSOR):
            to = ring(t, i, TENSOR)
            frm = ring(t, -i, TENSOR)
            got.append(
                xfer(pv.at[core, to, mine], pg.at[core, t, mine], pg.at[core, frm, mine], tpeer[i - 1])
            )
        yield
        for r in got:
            r.wait_recv()
        got = []
        for i in range(1, ZS):
            theirs = pl.ds(pl.multiple_of(ring(z, -i, ZS) * SH, 16), SH)
            block = pg.at[core, :, mine]
            got.append(xfer(block, block, pg.at[core, :, theirs], zpeer[i - 1]))
        yield
        for r in got:
            r.wait_recv()
        a = xfer(pg.at[core], pg.at[core], pg.at[1 - core], sibling)
        yield
        a.wait_recv()

    def sum_rewards():
        a = xfer(rt.at[0], rt.at[1], rt.at[1], sibling)
        yield
        a.wait_recv()
        rt[2] = rt[0] + rt[1]
        got = [xfer(rt.at[2], rt.at[2 + i], rt.at[2 + i], zpeer[i - 1]) for i in range(1, ZS)]
        yield
        for r in got:
            r.wait_recv()
        total = rt[2]
        for i in range(1, ZS):
            total = total + rt[2 + i]
        rt[10] = total
        a = xfer(rt.at[10], rt.at[11], rt.at[11], partner)
        yield
        a.wait_recv()

    def attention(r):
        length = lengths[2 * dp + r]
        srow = lax.broadcasted_iota(jnp.int32, (SLOTS, SLOTS), 0)
        tcol = lax.broadcasted_iota(jnp.int32, (SLOTS, SLOTS), 1)
        allowed = (srow <= tcol) & (srow < length)
        live = lax.broadcasted_iota(jnp.int32, (SLOTS, HEAD), 0) < length
        scale = 1.0 / math.sqrt(HEAD)
        dkv[r] = jnp.zeros((SLOTS, 2 * HEAD), F32)

        @pl.loop(0, HEADS)
        def _(h):
            cols = pl.ds(pl.multiple_of(h * HEAD, HEAD), HEAD)
            q = qv[r, :, cols]
            g = jnp.where(live, dov[r, :, cols].astype(F32), 0.0).astype(BF)
            k = kvv[r, :, 0:HEAD]
            v = kvv[r, :, HEAD : 2 * HEAD]
            s = jnp.where(allowed, dot(k, q, 1, 1) * scale, -1e30)
            e = jnp.exp(s - jnp.max(s, axis=0, keepdims=True))
            att = e * (1.0 / jnp.sum(e, axis=0, keepdims=True))
            w = dot(v, g, 1, 1)
            delta = jnp.sum(att * w, axis=0, keepdims=True)
            ds = (att * (w - delta)).astype(BF)
            dkv[r, :, 0:HEAD] += dot(ds, q, 1, 0) * scale
            dkv[r, :, HEAD : 2 * HEAD] += dot(att.astype(BF), g, 1, 0)
            dqf[r, :, cols] = dot(ds, k, 0, 0) * scale

    def finish_attention():
        total = rt[10] + rt[11]
        for r in range(2):
            mean = jnp.sum(jnp.where(group_row == groups[r], total, 0.0), axis=0, keepdims=True)[:, 0:1] / GROUP
            advantage = rewards[r] - mean
            dq_out[r] = (dqf[r] * advantage).astype(BF)
            kvown[r] = (dkv[r] * advantage).astype(BF)
        kvg[t] = kvown[...]
        kva[0] = kvown[kept]
        kvm[...] = kvown[gone]

    def gather_key_values():
        at = lambda idx, r: kvg.at[idx, r]
        a = xfer(kvg.at[t], kvg.at[t], kvg.at[pair_t], pair)
        up = [xfer(kvg.at[t], kvg.at[t], kvg.at[yt(-1)], yp)]
        down = [xfer(kvg.at[t], kvg.at[t], kvg.at[yt(1)], ym)]
        yield
        a.wait_recv()
        up.append(xfer(kvg.at[pair_t], kvg.at[pair_t], kvg.at[yt(-1, 1 - xl)], yp))
        down.append(xfer(kvg.at[pair_t], kvg.at[pair_t], kvg.at[yt(1, 1 - xl)], ym))
        last = []
        for i, x_ in ((0, xl), (1, 1 - xl)):
            yield
            up[i].wait_recv()
            p = at(yt(-1, x_), 0)
            last.append(xfer(p, p, at(yt(2, x_), 0), yp))
            down[i].wait_recv()
            p = at(yt(1, x_), 1)
            last.append(xfer(p, p, at(yt(2, x_), 1), ym))
        yield
        for r in last:
            r.wait_recv()

    rank, where = [], [jnp.int32(0)] * SYNCED
    seen = jnp.int32(0)
    for j in range(TENSOR):
        on = flags[j] == 1
        rank.append(jnp.minimum(seen, SYNCED - 1))
        for k in range(SYNCED):
            where[k] = jnp.where(on & (seen == k), j, where[k])
        seen = seen + jnp.where(on, 1, 0)

    def new_state(c0, cw):
        @pl.loop(0, TENSOR)
        def _(b):
            grad = dot(xg[b, 0, :, c0 : c0 + cw], kva[0], 0, 0) + dot(xg[b, 1, :, c0 : c0 + cw], kva[1], 0, 0)
            st[b, c0 : c0 + cw] = (0.9 * mv[b, c0 : c0 + cw].astype(F32) + 0.1 * grad).astype(BF)

    def average(c0, cw, sc, cr, ab, zr, xs, xr, mn):
        n = cw // 4
        for k in range(SYNCED):
            sc[k // 2, (k % 2) * cw : (k % 2 + 1) * cw] = st[where[k], c0 : c0 + cw]
        a = xfer(sc.at[1 - core], cr, cr, sibling)
        yield
        a.wait_recv()
        for i in range(ZS):
            rows = slice(i * n, (i + 1) * n)
            ab[i] = (sc[core, rows].astype(F32) + cr[rows].astype(F32)).astype(BF)
        got = [xfer(ab.at[ring(z, i, ZS)], zr.at[i - 1], zr.at[i - 1], zpeer[i - 1]) for i in range(1, ZS)]
        yield
        total = ab[z].astype(F32)
        for i in range(1, ZS):
            got[i - 1].wait_recv()
            total = total + zr[i - 1].astype(F32)
        xs[...] = total.astype(BF)
        a = xfer(xs, xr, xr, partner)
        yield
        a.wait_recv()
        mine = mn.at[core * 2 + z // 4, lax.rem(z, 4)]
        mn[core * 2 + z // 4, lax.rem(z, 4)] = (
            (xs[...].astype(F32) + xr[...].astype(F32)) * (1.0 / REPLICAS)
        ).astype(BF)
        got = []
        for i in range(1, ZS):
            other = ring(z, -i, ZS)
            got.append(xfer(mine, mine, mn.at[core * 2 + other // 4, lax.rem(other, 4)], zpeer[i - 1]))
        yield
        for r in got:
            r.wait_recv()
        half = mn.at[pl.ds(core * 2, 2)]
        a = xfer(half, half, mn.at[pl.ds((1 - core) * 2, 2)], sibling)
        yield
        a.wait_recv()
        for j in range(TENSOR):
            synced = mn[rank[j]].reshape(cw, 2 * HEAD)
            mom_out[j, c0 : c0 + cw] = jnp.where(flags[j] == 1, synced, st[j, c0 : c0 + cw])

    def input_gradient():
        @pl.loop(0, 6)
        def _(i):
            r = i // 3
            rows = pl.ds(pl.multiple_of(lax.rem(i, 3) * 128, 128), 128)
            total = jnp.zeros((128, WIDTH), F32)
            for b in range(TENSOR):
                for h in range(2):
                    total = total + dot(kvg[b, r, rows, h * 128 : (h + 1) * 128], pg[h, b], 1, 1)
            ig_out[r, rows] = total.astype(BF)

    def step(*generators):
        for g in generators:
            next(g, None)

    kept_g = [gather_kept(*c) for c in CHUNKS]
    moved_g = [gather_moved(*c) for c in CHUNKS]
    pro, rew = gather_projection(), sum_rewards()
    step(moved_g[0], kept_g[0], rew, pro)
    lkv.wait()
    lq.wait()
    ldo.wait()
    attention(0)
    step(rew, pro)
    attention(1)
    step(rew)
    step(moved_g[0], kept_g[0], pro)
    step(rew)
    finish_attention()
    swap = xfer(kvm, kva.at[1], kva.at[1], partner)
    step(moved_g[0], kept_g[0])
    step(moved_g[0], kept_g[0])
    step(moved_g[0])
    step(moved_g[0])
    kvs = gather_key_values()
    step(kvs, kvs)
    swap.wait_recv()
    lmom.wait()
    new_state(*CHUNKS[0])
    av = [average(*c, **ar[i]) for i, c in enumerate(CHUNKS)]
    step(av[0], av[0], kvs, pro, av[0], kvs, av[0], kvs, av[0])
    input_gradient()
    step(av[0])
    for copy in sent:
        copy.wait_send()


def shards(
    layer_input,
    queries,
    projected_key_value,
    output_grad,
    projection,
    moment,
    rewards,
    groups,
    lengths,
    assignment,
    sync_flags,
):
    any_spec = pl.BlockSpec(memory_space=pl.ANY)
    smem = pl.BlockSpec(memory_space=pltpu.SMEM)
    vmem = pl.BlockSpec(memory_space=pltpu.VMEM)
    scratch = [
        pltpu.VMEM((2, SLOTS, WIDTH), BF),
        pltpu.VMEM((2, SLOTS, WIDTH), BF),
        pltpu.VMEM((2, SLOTS, 2 * HEAD), BF),
        pltpu.VMEM((2, SLOTS, WIDTH), BF),
        pltpu.VMEM((2, TENSOR, WIDTH, HEAD), BF),
        pltpu.VMEM((2, TENSOR, WIDTH, HEAD), BF),
        pltpu.VMEM((TENSOR, WIDTH, 2 * HEAD), BF),
        pltpu.VMEM((TENSOR, 2, SLOTS, WIDTH), BF),
        pltpu.VMEM((SLOTS, WIDTH), BF),
        pltpu.VMEM((2, SLOTS, 2 * HEAD), BF),
        pltpu.VMEM((TENSOR, 2, SLOTS, 2 * HEAD), BF),
        pltpu.VMEM((2, SLOTS, 2 * HEAD), BF),
        pltpu.VMEM((SLOTS, 2 * HEAD), BF),
        pltpu.VMEM((TENSOR, WIDTH, 2 * HEAD), BF),
        pltpu.VMEM((2, SLOTS, WIDTH), F32),
        pltpu.VMEM((2, SLOTS, 2 * HEAD), F32),
        pltpu.VMEM((12, 8, 128), F32),
    ]
    for _, cw in CHUNKS:
        n = cw // 4
        scratch += [
            pltpu.VMEM((2, 2 * cw, 2 * HEAD), BF),
            pltpu.VMEM((2 * cw, 2 * HEAD), BF),
            pltpu.VMEM((ZS, n, 2 * HEAD), BF),
            pltpu.VMEM((ZS - 1, n, 2 * HEAD), BF),
            pltpu.VMEM((n, 2 * HEAD), BF),
            pltpu.VMEM((n, 2 * HEAD), BF),
            pltpu.VMEM((4, 4, n, 2 * HEAD), BF),
        ]
    scratch += [pltpu.SemaphoreType.DMA((SEMS,)), pltpu.SemaphoreType.DMA((SEMS,)), pltpu.SemaphoreType.DMA((8,))]
    dq, ig, out = pl.pallas_call(
        kernel,
        name="layer_back",
        out_shape=(
            jax.ShapeDtypeStruct((2, SLOTS, WIDTH), BF),
            jax.ShapeDtypeStruct((2, SLOTS, WIDTH), BF),
            jax.ShapeDtypeStruct((TENSOR, WIDTH, 2 * HEAD), BF),
        ),
        in_specs=[any_spec] * 6 + [smem] * 5,
        out_specs=(vmem, vmem, vmem),
        scratch_shapes=scratch,
        compiler_params=pltpu.CompilerParams(
            collective_id=0, has_side_effects=True, vmem_limit_bytes=56 * 2**20
        ),
        cost_estimate=pl.CostEstimate(flops=6 * 10**9, bytes_accessed=16 * 10**6, transcendentals=15 * 10**5),
    )(
        layer_input.reshape(2, SLOTS, WIDTH),
        queries.reshape(2, SLOTS, WIDTH),
        projected_key_value.reshape(2, SLOTS, 2 * HEAD),
        output_grad.reshape(2, SLOTS, WIDTH),
        projection.reshape(TENSOR, WIDTH, 2 * HEAD),
        moment.reshape(TENSOR, WIDTH, 2 * HEAD),
        rewards,
        groups,
        lengths,
        assignment,
        sync_flags,
    )
    return (
        dq.reshape(2 * SLOTS, WIDTH),
        ig.reshape(2 * SLOTS, WIDTH),
        out.reshape(1, TENSOR * WIDTH, 1, 2 * HEAD),
    )


def solution(mesh):
    return jax.shard_map(
        shards,
        mesh=mesh,
        in_specs=(
            P("dp", "tensor"),
            P("dp", "tensor"),
            P("dp", "tensor", None),
            P("dp", "tensor"),
            P(None, "tensor", None),
            P("dp", None, "tensor", None),
            P("dp"),
            P("dp"),
            P(),
            P(),
            P(),
        ),
        out_specs=(P("dp", "tensor"), P("dp", "tensor"), P("dp", None, "tensor", None)),
        check_vma=False,
    )
```

time: 761 us -> 150 us (0.20)
  waiting for transfers between devices: 580 us -> 0 us
  Pallas kernels: 0 us -> 143 us
  blocking collectives: 68.9 us -> 0 us
  local copies, waits for them, and re-layouts: 42.1 us -> 6.11 us
  other arithmetic: 29.2 us -> 0 us
  matrix products: 22.9 us -> 0 us
  between operations: 13.9 us -> 0.65 us
    psum x1 -> x0, waiting for transfers between devices: 268 us -> none  [shards(): summed = lax.psum(updated_state, 'dp').astype(jnp.float32)]
    unnamed x4 -> x0, waiting for transfers between devices: 153 us -> none
    pallas_call x0 -> x1, Pallas kernels: none -> 143 us  [shards(): pl.pallas_call(kernel, name='layer_back', out_shape=(jax.ShapeDtypeStruct...]
    all_gather x1 -> x0, waiting for transfers between devices: 124 us -> none  [weight_grads(): lax.all_gather(row_inputs, 'tensor', axis=1, tiled=True)]
    psum x1 -> x0, blocking collectives: 68.9 us -> none  [shards(): group_sums = lax.psum(jnp.sum(member * rewards[:, None], axis=0), 'dp')]
    ppermute x2 -> x0, waiting for transfers between devices: 34 us -> none  [swapped(): return lax.ppermute(value, axis, pairs)]
    dot_general x7 -> x0, matrix products: 22.9 us -> none  [the longest x1 7.82 us: weight_grads(): lax.dot_general(lax.all_gather(row_inputs, 'tensor', axis=1, tiled=True),...]
    slice x7 -> x0, local copies, waits for them, and re-layouts: 14.7 us -> none  [the longest x2 5.2 us: shards(): input_grad = restored[:, :, query_width:].reshape(tokens, feature_width)]
  transfers between devices with their start and end apart: 5 -> 0, of which waited for: 4 -> 0; matrix products, arithmetic and copies ran while one was open for 8% -> 0% of each run, Pallas kernels for 0% -> 0%
where the time goes in v1:
time: 150 us
  Pallas kernels  143 us (95%)
  local copies, waits for them, and re-layouts  6.11 us (4%)
    pallas_call x1, Pallas kernels, shards(): pl.pallas_call(kernel, name='layer_back', out_shape=(jax.ShapeDtypeStruct...  143 us
    unnamed x5, local copies, waits for them, and re-layouts  6.11 us

profile of v1, /device:TPU:1, one launch (start us, length us, event | category | flops | bytes accessed | tf_op | source)
XLA Modules:
  0.0 149.6 jit_solution(285319907805787303)
XLA Ops:
  0.6 142.8 %layer_back.1 = (bf16[2,384,640]{2,1,0:T(8,128)(2,1)}, bf16[2,384,640]{2,1,0:T(8,128)(2,1)}, bf16[8,640,256]{2,1,0:T(8,128)(2,1)}) custom-call(bf16[2,384,640]{2,1,0:T(8,128)(2,1)} %bitcast.14, bf16[2,384,640]{2,1,0:T(8,128)(2,1)} %bitcast.15, bf16[2,384,256]{2,1,0:T(8,128)(2,1)} %bitcast.17, bf16[2,384,640]{2,1,0:T(8,128)(2,1)} %bitcast.16, ...), custom_call_target="tpu_custom_call" | custom-call | flops 6000000000 | bytes 16000000 | tf_op jit(solution)/shard_map/layer_back/pallas_call | solution.py:411
  143.4 0.0 copy-start
  143.5 2.4 %copy.17 = bf16[768,640]{1,0:T(8,128)(2,1)} copy(bf16[768,640]{1,0:T(8,128)(2,1)} %bitcast.11) | data formatting | bytes 1966080
  145.8 2.2 %copy.18 = bf16[768,640]{1,0:T(8,128)(2,1)} copy(bf16[768,640]{1,0:T(8,128)(2,1)} %bitcast.10) | data formatting | bytes 1966080
  148.1 0.0 copy-done
  148.1 1.5 copy.19
Async XLA Ops:
  143.4 4.6 %copy-start = (bf16[8,640,256]{2,1,0:T(8,128)(2,1)S(1)}, bf16[8,640,256]{2,1,0:T(8,128)(2,1)}, u32[]{:S(2)}) copy-start(bf16[8,640,256]{2,1,0:T(8,128)(2,1)} %get-tuple-element.8) | copy-start | bytes 7864324

commit v2 on v1

--- a/solution.py
+++ b/solution.py
@@ -17,8 +17,8 @@
 WIDTH = 640
 GROUP = 8
 SYNCED = 4
-CHUNKS = ((0, 640),)
-SEMS = 128
+CHUNKS = ((0, 384), (384, 256))
+SEMS = 160
 BF = jnp.bfloat16
 F32 = jnp.float32
 MESH = pl.DeviceIdType.MESH
@@ -34,9 +34,9 @@
     take = lambda n: [refs.pop(0) for _ in range(n)]
     x_hbm, q_hbm, kv_hbm, do_hbm, proj_hbm, mom_hbm = take(6)
     rewards, groups, lengths, assignment, flags = take(5)
-    dq_out, ig_out, mom_out = take(3)
+    dq_hbm, ig_hbm, mom_hbm_out = take(3)
     xv, qv, kvv, dov, pv, pg, mv, xg, xm, kvown, kvg, kva, kvm, st, dqf, dkv = take(16)
-    rt = take(1)[0]
+    rt, igf, dq_out, ig_out, mom_out = take(5)
     ar = [dict(zip(("sc", "cr", "ab", "zr", "xs", "xr", "mn"), take(7))) for _ in range(nc)]
     ss, rs, ls = take(3)
 
@@ -117,17 +117,20 @@
         yield
         b.wait_recv()
         f = xfer(at(yt(-1), top), at(yt(-1), top), at(yt(2), top), yp)
-        d = xfer(at(yt(-1)), at(yt(-1)), at(yt(-1, 1 - xl)), pair)
         c.wait_recv()
         g = xfer(at(yt(1), low), at(yt(1), low), at(yt(2), low), ym)
+        yield
+        d = xfer(at(yt(-1)), at(yt(-1)), at(yt(-1, 1 - xl)), pair)
         e = xfer(at(yt(1)), at(yt(1)), at(yt(1, 1 - xl)), pair)
         yield
         f.wait_recv()
         g.wait_recv()
         h = xfer(at(yt(2)), at(yt(2)), at(yt(2, 1 - xl)), pair)
         yield
-        for r in (a, d, e, h):
-            r.wait_recv()
+        for r in (a, d, e):
+            r.wait_recv()
+        yield
+        h.wait_recv()
 
     def gather_moved(c0, cw):
         cols = pl.ds(c0, cw)
@@ -314,25 +317,36 @@
             synced = mn[rank[j]].reshape(cw, 2 * HEAD)
             mom_out[j, c0 : c0 + cw] = jnp.where(flags[j] == 1, synced, st[j, c0 : c0 + cw])
 
-    def input_gradient():
-        @pl.loop(0, 6)
-        def _(i):
-            r = i // 3
-            rows = pl.ds(pl.multiple_of(lax.rem(i, 3) * 128, 128), 128)
-            total = jnp.zeros((128, WIDTH), F32)
-            for b in range(TENSOR):
-                for h in range(2):
-                    total = total + dot(kvg[b, r, rows, h * 128 : (h + 1) * 128], pg[h, b], 1, 1)
-            ig_out[r, rows] = total.astype(BF)
+    def input_gradient(blocks, first, last):
+        @pl.loop(0, 2)
+        def _(r):
+            total = None if first else igf[r]
+            for b in blocks:
+                weight = jnp.concatenate([pg[0, b], pg[1, b]], axis=1)
+                term = dot(kvg[b, r], weight, 1, 1)
+                total = term if total is None else total + term
+            if last:
+                ig_out[r] = total.astype(BF)
+            else:
+                igf[r] = total
+
+    stores = []
+
+    def store(src, dst):
+        copy = pltpu.make_async_copy(src, dst, ls.at[7 + len(stores)])
+        copy.start()
+        stores.append(copy)
 
     def step(*generators):
         for g in generators:
             next(g, None)
 
-    kept_g = [gather_kept(*c) for c in CHUNKS]
-    moved_g = [gather_moved(*c) for c in CHUNKS]
+    k0, k1 = [gather_kept(*c) for c in CHUNKS]
+    m0, m1 = [gather_moved(*c) for c in CHUNKS]
+    a0, a1 = [average(*c, **ar[i]) for i, c in enumerate(CHUNKS)]
+    kvs = gather_key_values()
     pro, rew = gather_projection(), sum_rewards()
-    step(moved_g[0], kept_g[0], rew, pro)
+    step(m0, m1, k0, k1, rew, pro)
     lkv.wait()
     lq.wait()
     ldo.wait()
@@ -340,25 +354,51 @@
     step(rew, pro)
     attention(1)
     step(rew)
-    step(moved_g[0], kept_g[0], pro)
+    step(m0, m1, k0, k1)
     step(rew)
     finish_attention()
+    store(dq_out, dq_hbm)
     swap = xfer(kvm, kva.at[1], kva.at[1], partner)
-    step(moved_g[0], kept_g[0])
-    step(moved_g[0], kept_g[0])
-    step(moved_g[0])
-    step(moved_g[0])
-    kvs = gather_key_values()
-    step(kvs, kvs)
+    step(m0, k0, m1, k0)
+    step(pro)
+    step(m0, m0, m1, m1)
+    step(k0)
+    step(k1, k1)
+    step(kvs)
+    step(k0, m0)
     swap.wait_recv()
     lmom.wait()
     new_state(*CHUNKS[0])
-    av = [average(*c, **ar[i]) for i, c in enumerate(CHUNKS)]
-    step(av[0], av[0], kvs, pro, av[0], kvs, av[0], kvs, av[0])
-    input_gradient()
-    step(av[0])
+    step(a0, a0)
+    step(k1, k1, m1)
+    new_state(*CHUNKS[1])
+    step(a1, a0, a1)
+    step(kvs, pro, a0, kvs, a1, a0, a1, kvs)
+    input_gradient((t, pair_t, yt(-1), yt(1), yt(-1, 1 - xl), yt(1, 1 - xl)), True, False)
+    step(a0, a1)
+    step(kvs)
+    input_gradient((yt(2), yt(2, 1 - xl)), False, True)
+    store(ig_out, ig_hbm)
+    step(a1)
+    store(mom_out, mom_hbm_out)
+    for copy in stores:
+        copy.wait()
     for copy in sent:
         copy.wait_send()
+
+
+def place(dq, ig, out, dq_to, ig_to, out_to, dq_v, ig_v, out_v, sems):
+    parts = [(a.at[r], v.at[r], b.at[r]) for a, v, b in ((dq, dq_v, dq_to), (ig, ig_v, ig_to)) for r in range(2)]
+    parts += [(out.at[j], out_v.at[j], out_to.at[j]) for j in range(TENSOR)]
+    loads = [pltpu.make_async_copy(a, v, sems.at[0, i]) for i, (a, v, _) in enumerate(parts)]
+    stores = [pltpu.make_async_copy(v, b, sems.at[1, i]) for i, (_, v, b) in enumerate(parts)]
+    for load in loads:
+        load.start()
+    for load, store in zip(loads, stores):
+        load.wait()
+        store.start()
+    for store in stores:
+        store.wait()
 
 
 def shards(
@@ -376,7 +416,6 @@
 ):
     any_spec = pl.BlockSpec(memory_space=pl.ANY)
     smem = pl.BlockSpec(memory_space=pltpu.SMEM)
-    vmem = pl.BlockSpec(memory_space=pltpu.VMEM)
     scratch = [
         pltpu.VMEM((2, SLOTS, WIDTH), BF),
         pltpu.VMEM((2, SLOTS, WIDTH), BF),
@@ -395,6 +434,10 @@
         pltpu.VMEM((2, SLOTS, WIDTH), F32),
         pltpu.VMEM((2, SLOTS, 2 * HEAD), F32),
         pltpu.VMEM((12, 8, 128), F32),
+        pltpu.VMEM((2, SLOTS, WIDTH), F32),
+        pltpu.VMEM((2, SLOTS, WIDTH), BF),
+        pltpu.VMEM((2, SLOTS, WIDTH), BF),
+        pltpu.VMEM((TENSOR, WIDTH, 2 * HEAD), BF),
     ]
     for _, cw in CHUNKS:
         n = cw // 4
@@ -407,7 +450,7 @@
             pltpu.VMEM((n, 2 * HEAD), BF),
             pltpu.VMEM((4, 4, n, 2 * HEAD), BF),
         ]
-    scratch += [pltpu.SemaphoreType.DMA((SEMS,)), pltpu.SemaphoreType.DMA((SEMS,)), pltpu.SemaphoreType.DMA((8,))]
+    scratch += [pltpu.SemaphoreType.DMA((SEMS,)), pltpu.SemaphoreType.DMA((SEMS,)), pltpu.SemaphoreType.DMA((16,))]
     dq, ig, out = pl.pallas_call(
         kernel,
         name="layer_back",
@@ -417,7 +460,7 @@
             jax.ShapeDtypeStruct((TENSOR, WIDTH, 2 * HEAD), BF),
         ),
         in_specs=[any_spec] * 6 + [smem] * 5,
-        out_specs=(vmem, vmem, vmem),
+        out_specs=(any_spec,) * 3,
         scratch_shapes=scratch,
         compiler_params=pltpu.CompilerParams(
             collective_id=0, has_side_effects=True, vmem_limit_bytes=56 * 2**20
@@ -436,6 +479,14 @@
         assignment,
         sync_flags,
     )
+    dq, ig, out = pl.pallas_call(
+        place,
+        name="place",
+        out_shape=tuple(jax.ShapeDtypeStruct(a.shape, BF) for a in (dq, ig, out)),
+        in_specs=[any_spec] * 3,
+        out_specs=(any_spec,) * 3,
+        scratch_shapes=[pltpu.VMEM(a.shape, BF) for a in (dq, ig, out)] + [pltpu.SemaphoreType.DMA((2, 12))],
+    )(dq, ig, out)
     return (
         dq.reshape(2 * SLOTS, WIDTH),
         ig.reshape(2 * SLOTS, WIDTH),

time: 150 us -> 118 us (0.79)
  Pallas kernels: 143 us -> 117 us
  local copies, waits for them, and re-layouts: 6.11 us -> 0 us
    pallas_call x1, Pallas kernels: 143 us -> 113 us  [shards(): pl.pallas_call(kernel, name='layer_back', out_shape=(jax.ShapeDtypeStruct...]
    unnamed x5 -> x0, local copies, waits for them, and re-layouts: 6.11 us -> none
    pallas_call x0 -> x1, Pallas kernels: none -> 4.02 us  [shards(): pl.pallas_call(place, name='place', out_shape=tuple((jax.ShapeDtypeStruct...]
where the time goes in v2:
time: 118 us
  Pallas kernels  117 us (99%)
    pallas_call x1, Pallas kernels, shards(): pl.pallas_call(kernel, name='layer_back', out_shape=(jax.ShapeDtypeStruct...  113 us
    pallas_call x1, Pallas kernels, shards(): pl.pallas_call(place, name='place', out_shape=tuple((jax.ShapeDtypeStruct...  4.02 us

profile of v2, /device:TPU:1, one launch (start us, length us, event | category | flops | bytes accessed | tf_op | source)
XLA Modules:
  0.0 117.8 jit_solution(5511261066875188044)
XLA Ops:
  0.6 113.2 %layer_back.1 = (bf16[2,384,640]{2,1,0:T(8,128)(2,1)}, bf16[2,384,640]{2,1,0:T(8,128)(2,1)}, bf16[8,640,256]{2,1,0:T(8,128)(2,1)}) custom-call(bf16[2,384,640]{2,1,0:T(8,128)(2,1)} %bitcast.12, bf16[2,384,640]{2,1,0:T(8,128)(2,1)} %bitcast.13, bf16[2,384,256]{2,1,0:T(8,128)(2,1)} %bitcast.17, bf16[2,384,640]{2,1,0:T(8,128)(2,1)} %bitcast.14, ...), custom_call_target="tpu_custom_call" | custom-call | flops 6000000000 | bytes 16000000 | tf_op jit(solution)/shard_map/layer_back/pallas_call | solution.py:454
  113.8 4.0 %place.1 = (bf16[2,384,640]{2,1,0:T(8,128)(2,1)}, bf16[2,384,640]{2,1,0:T(8,128)(2,1)}, bf16[8,640,256]{2,1,0:T(8,128)(2,1)}) custom-call(bf16[2,384,640]{2,1,0:T(8,128)(2,1)} %get-tuple-element.9.dq, bf16[2,384,640]{2,1,0:T(8,128)(2,1)} %get-tuple-element.10.ig, bf16[8,640,256]{2,1,0:T(8,128)(2,1)} %get-tuple-element.11.out), custom_call_target="tpu_custom_call" | custom-call | tf_op jit(solution)/shard_map/place/pallas_call | solution.py:482

commit v3 on v2

--- a/solution.py
+++ b/solution.py
@@ -346,7 +346,7 @@
     a0, a1 = [average(*c, **ar[i]) for i, c in enumerate(CHUNKS)]
     kvs = gather_key_values()
     pro, rew = gather_projection(), sum_rewards()
-    step(m0, m1, k0, k1, rew, pro)
+    step(m0, k0, m1, k1, rew, pro)
     lkv.wait()
     lq.wait()
     ldo.wait()
@@ -360,7 +360,6 @@
     store(dq_out, dq_hbm)
     swap = xfer(kvm, kva.at[1], kva.at[1], partner)
     step(m0, k0, m1, k0)
-    step(pro)
     step(m0, m0, m1, m1)
     step(k0)
     step(k1, k1)
@@ -373,7 +372,7 @@
     step(k1, k1, m1)
     new_state(*CHUNKS[1])
     step(a1, a0, a1)
-    step(kvs, pro, a0, kvs, a1, a0, a1, kvs)
+    step(kvs, a0, pro, kvs, a1, a0, a1, kvs, pro)
     input_gradient((t, pair_t, yt(-1), yt(1), yt(-1, 1 - xl), yt(1, 1 - xl)), True, False)
     step(a0, a1)
     step(kvs)

time: 118 us -> 118 us (level)
  no operation moved by 1% of the time
where the time goes in v3:
time: 118 us
  Pallas kernels  117 us (99%)
    pallas_call x1, Pallas kernels, shards(): pl.pallas_call(kernel, name='layer_back', out_shape=(jax.ShapeDtypeStruct...  113 us
    pallas_call x1, Pallas kernels, shards(): pl.pallas_call(place, name='place', out_shape=tuple((jax.ShapeDtypeStruct...  4.02 us

profile of v3, /device:TPU:1, one launch (start us, length us, event | category | flops | bytes accessed | tf_op | source)
XLA Modules:
  0.0 117.8 jit_solution(18129692604856390427)
XLA Ops:
  0.6 113.1 %layer_back.1 = (bf16[2,384,640]{2,1,0:T(8,128)(2,1)}, bf16[2,384,640]{2,1,0:T(8,128)(2,1)}, bf16[8,640,256]{2,1,0:T(8,128)(2,1)}) custom-call(bf16[2,384,640]{2,1,0:T(8,128)(2,1)} %bitcast.12, bf16[2,384,640]{2,1,0:T(8,128)(2,1)} %bitcast.13, bf16[2,384,256]{2,1,0:T(8,128)(2,1)} %bitcast.17, bf16[2,384,640]{2,1,0:T(8,128)(2,1)} %bitcast.14, ...), custom_call_target="tpu_custom_call" | custom-call | flops 6000000000 | bytes 16000000 | tf_op jit(solution)/shard_map/layer_back/pallas_call | solution.py:453
  113.8 4.0 %place.1 = (bf16[2,384,640]{2,1,0:T(8,128)(2,1)}, bf16[2,384,640]{2,1,0:T(8,128)(2,1)}, bf16[8,640,256]{2,1,0:T(8,128)(2,1)}) custom-call(bf16[2,384,640]{2,1,0:T(8,128)(2,1)} %get-tuple-element.9.dq, bf16[2,384,640]{2,1,0:T(8,128)(2,1)} %get-tuple-element.10.ig, bf16[8,640,256]{2,1,0:T(8,128)(2,1)} %get-tuple-element.11.out), custom_call_target="tpu_custom_call" | custom-call | tf_op jit(solution)/shard_map/place/pallas_call | solution.py:481
